TPU v7x, 32 devices: a whole 2x2x4 slice. The times are simulated.
32 devices in a mesh: img: 4 (over x, core), row: 8 (over z, y).
Axes of the slice: x: 2, y: 2, z: 4, core: 2. Of those that a mesh axis runs over, the one named last changes fastest.
Arguments:
- feats2: bfloat16 [32, 64, 16, 256], P('img', 'row'), may hold values from -6 to 6
- feats3: bfloat16 [32, 32, 8, 512], P(('img', 'row')), may hold values from -6 to 6
- match2: int32 [32, 3, 64, 16], P('img', None, 'row'), may hold values 0 or 1
- target2: float32 [32, 12, 64, 16], P('img', None, 'row'), may hold values from -6 to 6
- match3: int32 [32, 3, 32, 8], P(('img', 'row')), may hold values 0 or 1
- target3: float32 [32, 12, 32, 8], P(('img', 'row')), may hold values from -6 to 6
- positives: int32 [], replicated, may hold values from 6144 to 10239
- step_count: int32 [], replicated, may hold values from 1 to 20
- lat2_w: float32 [256, 256], replicated, may hold values from -0.375 to 0.375
- lat2_m: float32 [256, 256], replicated, may hold values from -0.0007324219 to 0.0007324219
- lat2_v: float32 [256, 256], replicated, may hold values from 6.510417e-08 to 2.6041667e-07
- lat3_w: float32 [512, 256], replicated, may hold values from -0.25 to 0.25
- lat3_m: float32 [512, 256], replicated, may hold values from -0.0007324219 to 0.0007324219
- lat3_v: float32 [512, 256], replicated, may hold values from 6.510417e-08 to 2.6041667e-07
- conv_w: float32 [2, 2304, 256], replicated, may hold values from -0.125 to 0.125
- conv_m: float32 [2, 2304, 256], replicated, may hold values from -0.0007324219 to 0.0007324219
- conv_v: float32 [2, 2304, 256], replicated, may hold values from 6.510417e-08 to 2.6041667e-07
- head_w: float32 [257, 12], replicated, may hold values from -0.375 to 0.375
- head_m: float32 [257, 12], replicated, may hold values from -0.00390625 to 0.00390625
- head_v: float32 [257, 12], replicated, may hold values from 1.6276042e-06 to 6.510417e-06
- bias_w: float32 [4, 256], replicated, may hold values from -1.5 to 1.5
- bias_m: float32 [4, 256], replicated, may hold values from -0.0024414062 to 0.0024414062
- bias_v: float32 [4, 256], replicated, may hold values from 5.859375e-07 to 2.34375e-06
Outputs:
- loss: float32 [], replicated
- lat2_new: float32 [256, 256], replicated
- lat2_m_new: float32 [256, 256], replicated
- lat2_v_new: float32 [256, 256], replicated
- lat2_copy: bfloat16 [256, 256], replicated
- lat3_new: float32 [512, 256], replicated
- lat3_m_new: float32 [512, 256], replicated
- lat3_v_new: float32 [512, 256], replicated
- lat3_copy: bfloat16 [512, 256], replicated
- conv_new: float32 [2, 2304, 256], replicated
- conv_m_new: float32 [2, 2304, 256], replicated
- conv_v_new: float32 [2, 2304, 256], replicated
- conv_copy: bfloat16 [2, 2304, 256], replicated
- head_new: float32 [257, 12], replicated
- head_m_new: float32 [257, 12], replicated
- head_v_new: float32 [257, 12], replicated
- head_copy: bfloat16 [257, 12], replicated
- bias_new: float32 [4, 256], replicated
- bias_m_new: float32 [4, 256], replicated
- bias_v_new: float32 [4, 256], replicated
- bias_copy: bfloat16 [4, 256], replicated
All inputs are finite; a program needn't handle non-finite values. No bound on the sum of `match2` or of `match3` on one device may be relied on, other than what follows from the above.
Results may differ from a plain program's by a relative error of at most 0.0045.
The roundings to bfloat16 on the way count: a program that leaves them out, or rounds other values in their place, can miss the bound.
Values may be sent and summed in bfloat16 or wider, within the bound.
A program may use at most 128 MiB of HBM per device.

v0:
```python
import jax
import jax.numpy as jnp
from jax import lax
from jax.sharding import PartitionSpec as P

BETA = 1.0 / 9.0
SPECS = ("NHWC", "HWIO", "NHWC")


def with_halo(block, sides, width):
    for axis, dim in sides:
        count = lax.axis_size(axis)
        forward = [(i, i + 1) for i in range(count - 1)]
        backward = [(target, source) for source, target in forward]
        low = lax.ppermute(
            lax.slice_in_dim(block, block.shape[dim] - width, None, axis=dim), axis, forward
        )
        high = lax.ppermute(lax.slice_in_dim(block, 0, width, axis=dim), axis, backward)
        block = jnp.concatenate([low, block, high], axis=dim)
    return block


def from_behind(block, axis, distance):
    devices = range(lax.axis_size(axis))
    route = [(i - distance, i) for i in devices if i - distance in devices]
    return lax.ppermute(block, axis, route)


def conv_forward(inputs, kernel, pad_rows):
    return lax.conv_general_dilated(
        inputs,
        kernel,
        (1, 1),
        ((pad_rows, pad_rows), (1, 1)),
        dimension_numbers=SPECS,
        preferred_element_type=jnp.float32,
    )


def conv_input_grad(grad_r, kernel, pad_rows):
    flipped = jnp.flip(kernel, (0, 1)).transpose(0, 1, 3, 2)
    return lax.conv_general_dilated(
        grad_r,
        flipped,
        (1, 1),
        ((pad_rows, pad_rows), (1, 1)),
        dimension_numbers=SPECS,
        preferred_element_type=jnp.float32,
    )


def conv_weight_grad(padded, grad_r):
    rows, cols = (grad_r.shape[1], grad_r.shape[2])
    pieces = []
    for shift_r in range(3):
        for shift_c in range(3):
            window = padded[:, shift_r : shift_r + rows, shift_c : shift_c + cols, :]
            pieces.append(
                jnp.einsum("nhwc,nhwo->co", window, grad_r, preferred_element_type=jnp.float32)
            )
    stacked = jnp.stack(pieces)
    return stacked.reshape(9 * stacked.shape[1], stacked.shape[2])


def head_terms(feat_r, head_r, head_bias, match, target, norm):
    pred = (
        jnp.einsum("nhwc,ck->nkhw", feat_r, head_r, preferred_element_type=jnp.float32)
        + head_bias[None, :, None, None]
    )
    weight = jnp.repeat(match.astype(jnp.float32), 4, axis=1)
    diff = pred - target
    size = jnp.abs(diff)
    loss_part = jnp.sum(
        weight * jnp.where(size < BETA, 0.5 * diff * diff / BETA, size - 0.5 * BETA)
    )
    dpred = (weight * jnp.clip(diff / BETA, -1.0, 1.0) / norm).astype(jnp.bfloat16)
    grad_rows = jnp.einsum("nhwc,nkhw->ck", feat_r, dpred, preferred_element_type=jnp.float32)
    grad_bias = jnp.sum(dpred, axis=(0, 2, 3), dtype=jnp.float32)
    dfeat = jnp.einsum("nkhw,ck->nhwc", dpred, head_r, preferred_element_type=jnp.float32)
    return (loss_part, grad_rows, grad_bias, dfeat)


def adamw(weight, first, second, grad, count):
    first_new = 0.9 * first + 0.1 * grad
    second_new = 0.95 * second + 0.05 * grad * grad
    first_hat = first_new / (1.0 - jnp.power(0.9, count))
    second_hat = second_new / (1.0 - jnp.power(0.95, count))
    weight_new = weight - 0.02 * (first_hat / (jnp.sqrt(second_hat) + 1e-08) + 0.1 * weight)
    return (weight_new, first_new, second_new, weight_new.astype(jnp.bfloat16))


def body(
    feats2,
    feats3,
    match2,
    target2,
    match3,
    target3,
    positives,
    step_count,
    lat2_w,
    lat2_m,
    lat2_v,
    lat3_w,
    lat3_m,
    lat3_v,
    conv_w,
    conv_m,
    conv_v,
    head_w,
    head_m,
    head_v,
    bias_w,
    bias_m,
    bias_v,
):
    norm = positives.astype(jnp.float32)
    width = lat2_w.shape[1]
    lat2_r = lat2_w.astype(jnp.bfloat16)
    lat3_r = lat3_w.astype(jnp.bfloat16)
    kernel = conv_w.astype(jnp.bfloat16).reshape(2, 3, 3, width, width)
    head_r = head_w[:-1].astype(jnp.bfloat16)
    head_bias = head_w[-1]
    top = (
        jnp.einsum("nhwc,cf->nhwf", feats3, lat3_r, preferred_element_type=jnp.float32) + bias_w[1]
    )
    top_r = top.astype(jnp.bfloat16)
    strips = lax.all_to_all(top_r, "row", split_axis=1, concat_axis=0, tiled=True)
    coarse_r = (conv_forward(top_r, kernel[1], 1) + bias_w[3]).astype(jnp.bfloat16)
    loss3, head_g3, hbias_g3, dcoarse = head_terms(
        coarse_r, head_r, head_bias, match3, target3, norm
    )
    enlarged = jnp.repeat(jnp.repeat(strips, 2, axis=1), 2, axis=2)
    merged = (
        jnp.einsum("nhwc,cf->nhwf", feats2, lat2_r, preferred_element_type=jnp.float32)
        + bias_w[0]
        + enlarged
    )
    merged_r = merged.astype(jnp.bfloat16)
    extended = with_halo(merged_r, (("row", 1),), 1)
    fine_r = (conv_forward(extended, kernel[0], 0) + bias_w[2]).astype(jnp.bfloat16)
    loss2, head_g2, hbias_g2, dfine = head_terms(fine_r, head_r, head_bias, match2, target2, norm)
    dfine_r = dfine.astype(jnp.bfloat16)
    padded = jnp.pad(extended, ((0, 0), (0, 0), (1, 1), (0, 0)))
    conv_g2 = conv_weight_grad(padded, dfine_r)
    out_g2 = jnp.sum(dfine_r, axis=(0, 1, 2), dtype=jnp.float32)
    dextended = conv_input_grad(dfine_r, kernel[0], 2)
    rows = dextended.shape[1] - 2
    from_below = from_behind(dextended[:, 0].astype(jnp.bfloat16), "row", -1).astype(jnp.float32)
    from_above = from_behind(dextended[:, rows + 1].astype(jnp.bfloat16), "row", 1).astype(
        jnp.float32
    )
    dmerged = dextended[:, 1 : rows + 1]
    dmerged = dmerged.at[:, rows - 1].add(from_below).at[:, 0].add(from_above)
    dmerged_r = dmerged.astype(jnp.bfloat16)
    lat2_g = jnp.einsum("nhwc,nhwf->cf", feats2, dmerged_r, preferred_element_type=jnp.float32)
    lat2_bias_g = jnp.sum(dmerged_r, axis=(0, 1, 2), dtype=jnp.float32)
    images, cols = (dmerged.shape[0], dmerged.shape[2])
    pooled = dmerged.reshape(images, rows // 2, 2, cols // 2, 2, width).sum(axis=(2, 4))
    dup = lax.all_to_all(
        pooled.astype(jnp.bfloat16), "row", split_axis=0, concat_axis=1, tiled=True
    )
    dcoarse_r = dcoarse.astype(jnp.bfloat16)
    padded3 = jnp.pad(top_r, ((0, 0), (1, 1), (1, 1), (0, 0)))
    conv_g3 = conv_weight_grad(padded3, dcoarse_r)
    out_g3 = jnp.sum(dcoarse_r, axis=(0, 1, 2), dtype=jnp.float32)
    dtop_r = (conv_input_grad(dcoarse_r, kernel[1], 1) + dup.astype(jnp.float32)).astype(
        jnp.bfloat16
    )
    lat3_g = jnp.einsum("nhwc,nhwf->cf", feats3, dtop_r, preferred_element_type=jnp.float32)
    lat3_bias_g = jnp.sum(dtop_r, axis=(0, 1, 2), dtype=jnp.float32)
    head_g = jnp.concatenate([head_g2 + head_g3, (hbias_g2 + hbias_g3)[None]], axis=0)
    loss_part = (loss2 + loss3) / norm
    lat2_g, lat3_g, conv_g2, conv_g3, head_g, lat2_bias_g, lat3_bias_g, out_g2, out_g3, loss = (
        lax.psum(
            (
                lat2_g,
                lat3_g,
                conv_g2,
                conv_g3,
                head_g,
                lat2_bias_g,
                lat3_bias_g,
                out_g2,
                out_g3,
                loss_part,
            ),
            ("img", "row"),
        )
    )
    conv_g = jnp.stack([conv_g2, conv_g3])
    bias_g = jnp.stack([lat2_bias_g, lat3_bias_g, out_g2, out_g3])
    count = step_count.astype(jnp.float32)
    outs = [loss]
    for weight, first, second, grad in (
        (lat2_w, lat2_m, lat2_v, lat2_g),
        (lat3_w, lat3_m, lat3_v, lat3_g),
        (conv_w, conv_m, conv_v, conv_g),
        (head_w, head_m, head_v, head_g),
        (bias_w, bias_m, bias_v, bias_g),
    ):
        outs.extend(adamw(weight, first, second, grad, count))
    return tuple(outs)


def solution(mesh):
    return jax.shard_map(
        body,
        mesh=mesh,
        in_specs=(
            P("img", "row", None, None),
            P(("img", "row"), None, None, None),
            P("img", None, "row", None),
            P("img", None, "row", None),
            P(("img", "row"), None, None, None),
            P(("img", "row"), None, None, None),
            P(),
            P(),
            P(),
            P(),
            P(),
            P(),
            P(),
            P(),
            P(),
            P(),
            P(),
            P(),
            P(),
            P(),
            P(),
            P(),
            P(),
        ),
        out_specs=(
            P(),
            P(),
            P(),
            P(),
            P(),
            P(),
            P(),
            P(),
            P(),
            P(),
            P(),
            P(),
            P(),
            P(),
            P(),
            P(),
            P(),
            P(),
            P(),
            P(),
            P(),
        ),
        check_vma=False,
    )
```

profile of v0, /device:TPU:0, one launch (start us, length us, event | category | flops | bytes accessed | tf_op | source)
XLA Modules:
  0.0 274.6 jit_solution(16110540682120943012)
XLA Ops:
  7.2 0.8 fusion.125
  8.0 2.0 fusion.25
  10.1 7.3 %all-to-all-start = ((bf16[1,32,8,256]{3,2,0,1:T(8,128)(2,1)}), bf16[1,32,8,256]{3,2,0,1:T(8,128)(2,1)S(1)}, u32[]{:S(2)}, u32[]{:S(2)}) async-start(bf16[1,32,8,256]{3,2,0,1:T(8,128)(2,1)} %bitcast.8), calls=%async_computation | async-start | bytes 262144 | tf_op jit(solution)/shard_map/all_to_all | solution.py:128
  18.8 2.6 convert_element_type.149
  22.4 2.7 fusion.24
  26.7 1.9 fusion.23
  28.6 1.8 fusion.22
  30.5 1.8 fusion.21
  32.3 1.8 fusion.20
  34.1 1.8 fusion.19
  36.0 1.8 fusion.18
  37.8 1.8 fusion.17
  39.6 1.8 fusion.16
  41.5 1.6 broadcast_in_dim.17
  43.1 1.9 convert_element_type.147
  46.0 1.3 collective-permute-start.1
  47.3 4.6 %collective-permute-start = (bf16[8,1,16,256]{3,2,1,0:T(8,128)(2,1)}, bf16[8,1,16,256]{3,2,1,0:T(8,128)(2,1)S(1)}, u32[]{:S(2)}, u32[]{:S(2)}) collective-permute-start(bf16[8,1,16,256]{3,2,1,0:T(8,128)(2,1)} %get-tuple-element.176), channel_id=1, source_target_pairs={{0,1},{1,2},{2,3},{3,4},{4,5},{5,6},{6,7},{8,9},{9,10},{10,11},{11... | collective-permute-start | bytes 196616 | tf_op jit(solution)/shard_map/ppermute | solution.py:15
  51.9 1.8 fusion.15
  54.2 2.2 copy.239
  57.3 1.4 fusion.3
  58.8 1.1 convert_reduce_fusion.2
  59.9 0.9 convert_reduce_fusion
  60.8 1.8 fusion.126
  62.6 1.3 collective-permute-start.2
  63.9 5.6 %collective-permute-start.3 = (bf16[8,16,256]{2,0,1:T(8,128)(2,1)S(1)}, bf16[8,16,256]{2,0,1:T(8,128)(2,1)S(1)}, u32[]{:S(2)}, u32[]{:S(2)}) collective-permute-start(bf16[8,16,256]{2,0,1:T(8,128)(2,1)S(1)} %get-tuple-element.172), channel_id=1, source_target_pairs={{0,1},{1,2},{2,3},{3,4},{4,5},{5,6},{6,7},{8,9},{9,10},{10,11},{11... | collective-permute-start | bytes 196616 | tf_op jit(solution)/shard_map/ppermute | solution.py:26
  73.0 1.2 copy-done.2
  75.0 6.0 %all-to-all-start.1 = ((bf16[8,4,8,256]{3,2,1,0:T(8,128)(2,1)}), bf16[8,4,8,256]{3,2,1,0:T(8,128)(2,1)S(1)}, u32[]{:S(2)}, u32[]{:S(2)}) async-start(bf16[8,4,8,256]{3,2,1,0:T(8,128)(2,1)} %copy.254), calls=%async_computation.1 | async-start | bytes 262144 | tf_op jit(solution)/shard_map/all_to_all | solution.py:160
  81.1 1.3 convolution_bitcast_fusion.10
  82.4 6.0 %all-to-all-done.1 = bf16[8,4,8,256]{3,2,1,0:T(8,128)(2,1)S(1)} async-done(((bf16[8,4,8,256]{3,2,1,0:T(8,128)(2,1)}), bf16[8,4,8,256]{3,2,1,0:T(8,128)(2,1)S(1)}, u32[]{:S(2)}, u32[]{:S(2)}) %all-to-all-start.1) | async-done | bytes 131104 | tf_op jit(solution)/shard_map/all_to_all | solution.py:160
  88.7 2.5 convert_reduce_fusion.4
  91.2 1.1 convolution_bitcast_fusion
  92.3 0.8 copy.250
  94.3 1.8 copy.248
  96.1 1.9 copy.244
  98.2 1.2 copy.251
  102.0 1.4 convolution_bitcast_fusion.21
  103.4 1.1 fusion.28
  104.7 40.2 %all-reduce.2 = (f32[]{:T(128)}, f32[257,12]{0,1:T(8,128)S(1)}, f32[1,256]{1,0:T(1,128)S(1)}, f32[1,256]{1,0:T(1,128)S(1)}, f32[1,256]{1,0:T(1,128)S(1)}, /*index=5*/f32[1,256]{1,0:T(1,128)S(1)}) all-reduce(f32[]{:T(128)S(6)} %div.94, f32[257,12]{0,1:T(8,128)S(1)} %pad_maximum_fusion.3, ...), channel_id=1, replica_groups=mesh['img'=4,'row'=8] {'img','row'}, use_global_device_ids=true, to_apply=%region_2.3 | all-reduce | flops 4109 | bytes 32872 | tf_op jit(solution)/shard_map/psum | solution.py:175
  145.0 1.3 fusion.113
  147.0 95.3 %all-reduce.6.cloned.1.call-done = (f32[256,256]{0,1:T(8,128)}, f32[512,256]{0,1:T(8,128)}, f32[1,2304,256]{2,1,0:T(8,128)}, f32[1,2304,256]{2,1,0:T(8,128)}) async-done(((f32[256,256]{0,1:T(8,128)}, f32[512,256]{0,1:T(8,128)}, f32[1,2304,256]{2,1,0:T(8,128)}, f32[1,2304,256]{2,1,0:T(8,128)}), (f32[256,256]{0,1:T(8,128)}, f32[512,256]{0,1:T(8,128)}, f32[1,2304,256]{2,1,0:T(8,128)}, ...) | async-done | bytes 5505040 | tf_op jit(solution)/shard_map/psum | solution.py:175
  242.3 1.4 fusion.121
  246.9 2.3 fusion.119
  249.3 1.0 copy.282
  250.2 2.1 copy.283
  252.3 1.0 copy.284
  253.3 1.9 copy.285
  255.3 2.0 constant_dynamic-update-slice_fusion.1
  258.2 9.5 %fusion.117 = (bf16[2,2304,256]{2,1,0:T(8,128)(2,1)}, f32[2,2304,256]{2,1,0:T(8,128)}, f32[2,2304,256]{2,1,0:T(8,128)}, f32[2,2304,256]{2,1,0:T(8,128)}) fusion(f32[2,2304,256]{2,1,0:T(8,128)S(1)} %bitcast.275, f32[]{:T(128)S(6)} %sub.48, f32[]{:T(128)S(6)} %sub.47, f32[2,2304,256]{2,1,0:T(8,128)S(1)} %constant_dynamic-update-slice_fusion, ...), kind=kLoop, calls=%fused_computation.192 | loop fusion | flops 18874368 | bytes 35389448 | tf_op jit(solution)/shard_map/convert_element_type | solution.py:89
  (114 shorter events, 17.0 us)
Async XLA Ops:
  7.2 37.8 %copy-start = (bf16[8,8,16,256]{3,2,1,0:T(8,128)(2,1)S(1)}, bf16[8,8,16,256]{3,2,1,0:T(8,128)(2,1)}, u32[]{:S(2)}) copy-start(bf16[8,8,16,256]{3,2,1,0:T(8,128)(2,1)} %param.27) | copy-start | bytes 1572868
  10.1 31.4 %all-to-all-start = ((bf16[1,32,8,256]{3,2,0,1:T(8,128)(2,1)}), bf16[1,32,8,256]{3,2,0,1:T(8,128)(2,1)S(1)}, u32[]{:S(2)}, u32[]{:S(2)}) async-start(bf16[1,32,8,256]{3,2,0,1:T(8,128)(2,1)} %bitcast.8), calls=%async_computation | async-start | bytes 262144 | tf_op jit(solution)/shard_map/all_to_all | solution.py:128
  21.4 0.7 copy-start.26
  21.4 0.9 copy-start.23
  22.1 3.9 %copy-start.4 = (bf16[1,2304,256]{2,1,0:T(8,128)(2,1)}, bf16[1,2304,256]{2,1,0:T(8,128)(2,1)S(1)}, u32[]{:S(2)}) copy-start(bf16[1,2304,256]{2,1,0:T(8,128)(2,1)S(1)} %get-tuple-element.163) | copy-start | bytes 3538948
  22.1 3.0 %copy-start.15 = (f32[257,12]{0,1:T(8,128)S(1)}, f32[257,12]{0,1:T(8,128)}, u32[]{:S(2)}) copy-start(f32[257,12]{0,1:T(8,128)} %param.44) | copy-start | bytes 37012
  25.1 3.5 %copy-start.22 = (bf16[1,32,8,256]{3,0,2,1:T(2,128)(2,1)}, bf16[1,32,8,256]{3,0,2,1:T(2,128)(2,1)S(1)}, u32[]{:S(2)}) copy-start(bf16[1,32,8,256]{3,0,2,1:T(2,128)(2,1)S(1)} %fusion.24) | copy-start | bytes 393220
  26.0 4.5 %copy-start.12 = (bf16[1,12,32,8]{1,3,2,0:T(8,128)(2,1)}, bf16[1,12,32,8]{1,3,2,0:T(8,128)(2,1)S(1)}, u32[]{:S(2)}) copy-start(bf16[1,12,32,8]{1,3,2,0:T(8,128)(2,1)S(1)} %get-tuple-element.160) | copy-start | bytes 18436
  26.7 12.9 %copy-start.18 = (bf16[32,8,256]{2,1,0:T(8,128)(2,1)}, bf16[32,8,256]{2,1,0:T(8,128)(2,1)S(1)}, u32[]{:S(2)}) copy-start(bf16[32,8,256]{2,1,0:T(8,128)(2,1)S(1)} %get-tuple-element.184) | copy-start | bytes 393220
  41.5 3.6 %copy-start.6 = (f32[256,256]{1,0:T(8,128)S(1)}, f32[256,256]{1,0:T(8,128)}, u32[]{:S(2)}) copy-start(f32[256,256]{1,0:T(8,128)} %param.35) | copy-start | bytes 786436
  45.0 6.9 %copy-start.19 = (bf16[32,8,256]{2,1,0:T(8,128)(2,1)S(1)}, bf16[32,8,256]{2,1,0:T(8,128)(2,1)}, u32[]{:S(2)}) copy-start(bf16[32,8,256]{2,1,0:T(8,128)(2,1)} %copy-done.18) | copy-start | bytes 393220
  45.3 8.4 %copy-start.21 = (s32[8,3,8,16]{3,2,1,0:T(8,128)S(1)}, s32[8,3,8,16]{3,2,1,0:T(8,128)}, u32[]{:S(2)}) copy-start(s32[8,3,8,16]{3,2,1,0:T(8,128)} %param.29) | copy-start | bytes 36868
  46.0 10.4 %collective-permute-start.1 = (bf16[8,1,16,256]{3,2,1,0:T(8,128)(2,1)}, bf16[8,1,16,256]{3,2,1,0:T(8,128)(2,1)S(1)}, u32[]{:S(2)}, u32[]{:S(2)}) collective-permute-start(bf16[8,1,16,256]{3,2,1,0:T(8,128)(2,1)} %get-tuple-element.177), channel_id=1, source_target_pairs={{1,0},{2,1},{3,2},{4,3},{5,4},{6,5},{7,6},{9,8},{10,9},{11,10},{12... | collective-permute-start | bytes 196616 | tf_op jit(solution)/shard_map/ppermute | solution.py:18
  47.3 9.2 %collective-permute-start = (bf16[8,1,16,256]{3,2,1,0:T(8,128)(2,1)}, bf16[8,1,16,256]{3,2,1,0:T(8,128)(2,1)S(1)}, u32[]{:S(2)}, u32[]{:S(2)}) collective-permute-start(bf16[8,1,16,256]{3,2,1,0:T(8,128)(2,1)} %get-tuple-element.176), channel_id=1, source_target_pairs={{0,1},{1,2},{2,3},{3,4},{4,5},{5,6},{6,7},{8,9},{9,10},{10,11},{11... | collective-permute-start | bytes 196616 | tf_op jit(solution)/shard_map/ppermute | solution.py:15
  57.3 1.5 copy-start.9
  57.3 1.5 copy-start.16
  58.8 2.0 copy-start.11
  59.9 2.7 copy-start.7
  62.6 10.3 %collective-permute-start.2 = (bf16[8,16,256]{2,0,1:T(8,128)(2,1)S(1)}, bf16[8,16,256]{2,0,1:T(8,128)(2,1)S(1)}, u32[]{:S(2)}, u32[]{:S(2)}) collective-permute-start(bf16[8,16,256]{2,0,1:T(8,128)(2,1)S(1)} %get-tuple-element.173), channel_id=1, source_target_pairs={{1,0},{2,1},{3,2},{4,3},{5,4},{6,5},{7,6},{9,8},{10,9},{11,10},{12... | collective-permute-start | bytes 196616 | tf_op jit(solution)/shard_map/ppermute | solution.py:26
  63.9 9.1 %collective-permute-start.3 = (bf16[8,16,256]{2,0,1:T(8,128)(2,1)S(1)}, bf16[8,16,256]{2,0,1:T(8,128)(2,1)S(1)}, u32[]{:S(2)}, u32[]{:S(2)}) collective-permute-start(bf16[8,16,256]{2,0,1:T(8,128)(2,1)S(1)} %get-tuple-element.172), channel_id=1, source_target_pairs={{0,1},{1,2},{2,3},{3,4},{4,5},{5,6},{6,7},{8,9},{9,10},{10,11},{11... | collective-permute-start | bytes 196616 | tf_op jit(solution)/shard_map/ppermute | solution.py:26
  72.8 1.4 copy-start.2
  75.0 13.3 %all-to-all-start.1 = ((bf16[8,4,8,256]{3,2,1,0:T(8,128)(2,1)}), bf16[8,4,8,256]{3,2,1,0:T(8,128)(2,1)S(1)}, u32[]{:S(2)}, u32[]{:S(2)}) async-start(bf16[8,4,8,256]{3,2,1,0:T(8,128)(2,1)} %copy.254), calls=%async_computation.1 | async-start | bytes 262144 | tf_op jit(solution)/shard_map/all_to_all | solution.py:160
  81.0 7.6 %copy-start.5 = (bf16[1,2304,256]{2,1,0:T(8,128)(2,1)S(1)}, bf16[1,2304,256]{2,1,0:T(8,128)(2,1)}, u32[]{:S(2)}) copy-start(bf16[1,2304,256]{2,1,0:T(8,128)(2,1)} %copy-done.4) | copy-start | bytes 3538948
  81.0 7.6 %copy-start.20 = (bf16[32,8,256]{2,1,0:T(8,128)(2,1)S(1)}, bf16[32,8,256]{2,1,0:T(8,128)(2,1)}, u32[]{:S(2)}) copy-start(bf16[32,8,256]{2,1,0:T(8,128)(2,1)} %copy-done.18) | copy-start | bytes 393220
  81.1 161.2 %all-reduce.6.cloned.1.call-start = ((), (), s32[]{:S(2)}) async-start(), calls=%async_computation.2 | async-start | bytes 11010048 | tf_op jit(solution)/shard_map/psum | solution.py:175
  88.7 2.6 copy-start.14
  92.3 1.0 copy-start.3
  92.3 5.6 %copy-start.10 = (f32[512,256]{1,0:T(8,128)S(1)}, f32[512,256]{1,0:T(8,128)}, u32[]{:S(2)}) copy-start(f32[512,256]{1,0:T(8,128)} %param.40) | copy-start | bytes 1572868
  93.3 7.4 %copy-start.27 = (f32[12]{0:T(128)S(1)}, f32[12]{0:T(128)}, u32[]{:S(2)}) copy-start(f32[12]{0:T(128)} %get-tuple-element.159) | copy-start | bytes 148
  93.3 7.4 %copy-start.28 = (f32[12]{0:T(128)S(1)}, f32[12]{0:T(128)}, u32[]{:S(2)}) copy-start(f32[12]{0:T(128)} %get-tuple-element.161) | copy-start | bytes 148
  93.3 8.7 %copy-start.8 = (bf16[8,12,8,16]{1,3,2,0:T(8,128)(2,1)S(1)}, bf16[8,12,8,16]{1,3,2,0:T(8,128)(2,1)}, u32[]{:S(2)}) copy-start(bf16[8,12,8,16]{1,3,2,0:T(8,128)(2,1)} %copy-done.7) | copy-start | bytes 73732
  93.3 10.1 %copy-start.13 = (bf16[1,12,32,8]{1,3,2,0:T(8,128)(2,1)S(1)}, bf16[1,12,32,8]{1,3,2,0:T(8,128)(2,1)}, u32[]{:S(2)}) copy-start(bf16[1,12,32,8]{1,3,2,0:T(8,128)(2,1)} %copy-done.12) | copy-start | bytes 18436
  96.1 50.2 %copy-start.17 = (f32[257,12]{0,1:T(8,128)S(1)}, f32[257,12]{0,1:T(8,128)}, u32[]{:S(2)}) copy-start(f32[257,12]{0,1:T(8,128)} %param.44) | copy-start | bytes 37012
  96.1 50.2 %copy-start.24 = (f32[257,12]{0,1:T(8,128)S(1)}, f32[257,12]{0,1:T(8,128)}, u32[]{:S(2)}) copy-start(f32[257,12]{0,1:T(8,128)} %param.46) | copy-start | bytes 37012
  96.1 50.3 %copy-start.25 = (f32[257,12]{0,1:T(8,128)S(1)}, f32[257,12]{0,1:T(8,128)}, u32[]{:S(2)}) copy-start(f32[257,12]{0,1:T(8,128)} %param.45) | copy-start | bytes 37012
  250.2 7.2 %slice-start = ((s8[4718592]{0:T(1024)(128)(4,1)}), s8[524288]{0:T(1024)(128)(4,1)S(1)}, s32[]{:S(2)}) async-start(s8[4718592]{0:T(1024)(128)(4,1)} %bitcast.274), calls=%async_computation.3 | async-start | bytes 1048576
  253.3 3.9 %copy-start.1 = (f32[1,2304,256]{2,1,0:T(8,128)S(1)}, f32[1,2304,256]{2,1,0:T(8,128)}, u32[]{:S(2)}) copy-start(f32[1,2304,256]{2,1,0:T(8,128)} %get-tuple-element.138) | copy-start | bytes 7077892
  255.3 2.9 %slice-start.1 = ((s8[4718592]{0:T(1024)(128)(4,1)}), s8[4194304]{0:T(1024)(128)(4,1)S(1)}, s32[]{:S(2)}) async-start(s8[4718592]{0:T(1024)(128)(4,1)} %bitcast.274), calls=%async_computation.4 | async-start | bytes 8388608
Sparse Core Ops, SparseCore 0:
  92.4 149.7 all-reduce.5
where the time goes:
time: 276 us; the launch traced here: 275 us
  waiting for transfers between devices  101 us (37%)
  blocking collectives  40.2 us (15%)
  matrix products  38.9 us (14%)
  local copies, waits for them, and re-layouts  31.8 us (12%)
  starting transfers between devices  26.1 us (9%)
  other arithmetic  18.8 us (7%)
  between operations  17.3 us (6%)
    psum x1, waiting for transfers between devices, body(): lax.psum((lat2_g, lat3_g, conv_g2, conv_g3, head_g, lat2_bias_g, lat3_bia...  95.3 us
    psum x1, blocking collectives, body(): lax.psum((lat2_g, lat3_g, conv_g2, conv_g3, head_g, lat2_bias_g, lat3_bia...  40.2 us
    unnamed x79, local copies, waits for them, and re-layouts  22.6 us
    dot_general x18, matrix products, conv_weight_grad(): jnp.einsum('nhwc,nhwo->co', window, grad_r, preferred_element_type=jnp.fl...  19.7 us
    convert_element_type x5, other arithmetic, adamw(): return (weight_new, first_new, second_new, weight_new.astype(jnp.bfloat16))  15.3 us
    all_to_all x1, starting transfers between devices, body(): lax.all_to_all(top_r, 'row', split_axis=1, concat_axis=0, tiled=True)  7.29 us
    ppermute x2, starting transfers between devices, from_behind(): return lax.ppermute(block, axis, route)  6.91 us
    all_to_all x1, waiting for transfers between devices, body(): lax.all_to_all(pooled.astype(jnp.bfloat16), 'row', split_axis=0, concat_a...  6.01 us
  transfers between devices with their start and end apart: 7, of which 2 were waited for; matrix products, arithmetic and copies ran while one was open for 16% of the time, Pallas kernels for 0%

commit v1 on v0

v1 whole, which is shorter than its diff:
```python
import functools

import jax
import jax.numpy as jnp
from jax import lax
from jax.experimental import pallas as pl
from jax.experimental.pallas import tpu as pltpu
from jax.sharding import PartitionSpec as P

BETA = 1.0 / 9.0
MESH = pl.DeviceIdType.MESH
VMEM = pltpu.MemorySpace.VMEM
SMEM = pltpu.MemorySpace.SMEM
HBM = pltpu.MemorySpace.HBM
BF = jnp.bfloat16
F32 = jnp.float32
LANES = 128
TAP = 256
BLOCK = 256
TAPS = 21
FINE_JOBS = (
    (range(0, 5), ("x", "b", "a")),
    (range(5, 9), ("b", "x", "a")),
    (range(9, 12), ("x", "ba")),
    (range(12, 15), ("b", "xa")),
    (range(15, 18), ("x", "ba")),
    (range(18, 21), ("b", "xa")),
)
SCHEDULE = {
    "dtop3": (0, 1),
    "target": (),
    "strips": (0, 1),
    "enlarged": (),
    "merged": (),
    "inner": (0, 1),
    "forward": (0, 1),
    "backward": (),
    "conv2a": (),
    "conv2b": (2,),
    "conv2": (0, 1, 3),
    "lat2": (4, 2),
    "lat3": (0, 1, 3, 4, 2, 5),
}
LARGE_JOBS = (
    (range(0, 8), ("x", "b", "a")),
    (range(8, 16), ("b", "x", "a")),
    (range(16, 21), ("x", "b", "a")),
)
TINY = 24


class Plan:
    def __init__(self, mesh_shape, feats2, feats3):
        self.nimg, self.nrow = mesh_shape["img"], mesh_shape["row"]
        self.images, self.rows, self.cols, self.width = feats2
        self.high3, self.cols3, self.width3 = feats3[1:]
        self.strip = self.high3 // self.nrow
        self.lanes = self.images * self.cols
        self.cells3 = self.high3 * self.cols3
        minor = 1
        while minor * minor * 4 <= self.nrow:
            minor *= 2
        self.size = {"c": 2, "x": self.nimg // 2, "b": minor, "a": self.nrow // minor}
        grain = 16 * self.size["x"] * self.nrow
        self.jobs = FINE_JOBS if grain <= TAP else LARGE_JOBS
        self.start, self.length, self.tap_row, self.tap_job = [], [], {}, {}
        row = 0
        for number, (taps, _) in enumerate(self.jobs):
            self.start.append(row)
            for place, tap in enumerate(taps):
                self.tap_row[tap] = row + place * TAP
                self.tap_job[tap] = number
            self.length.append(-(-len(taps) * TAP // grain) * grain)
            row += self.length[-1]
        self.total = row
        self.tiny_links = sum(self.size.values()) - 4
        self.links = 1 + max(
            sum(self.count(group) - 1 for group in order) for _, order in self.jobs
        )

    def count(self, group):
        number = 1
        for dim in group:
            number *= self.size[dim]
        return number


class Place:
    def __init__(self, plan):
        self.plan = plan
        self.img, self.row = lax.axis_index("img"), lax.axis_index("row")
        minor = plan.size["b"]
        self.at = {
            "c": lax.rem(self.img, 2),
            "x": self.img // 2,
            "b": lax.rem(self.row, minor),
            "a": self.row // minor,
        }

    def moved(self, group, distance):
        at = dict(self.at)
        for dim in group[::-1]:
            size = self.plan.size[dim]
            step, distance = distance % size, distance // size
            if step:
                at[dim] = lax.rem(at[dim] + step, size)
        return at

    def coord(self, group, distance=0):
        at = self.moved(group, distance)
        number = 0
        for dim in group:
            number = number * self.plan.size[dim] + at[dim]
        return number

    def peer(self, group, distance):
        at = self.moved(group, distance)
        return (at["x"] * 2 + at["c"], at["a"] * self.plan.size["b"] + at["b"])

    def in_row(self, distance):
        return lax.rem(self.row + distance + self.plan.nrow, self.plan.nrow)


def when(condition, work):
    if condition is None:
        work()
    else:
        pl.when(condition)(work)


class Transfer:
    def __init__(self, copy, remote, out_if=None, in_if=None):
        self.copy, self.remote, self.out_if, self.in_if = copy, remote, out_if, in_if
        self.landed = self.left = False
        when(out_if, copy.start)

    def wait(self):
        if not self.landed:
            when(self.in_if, self.copy.wait_recv if self.remote else self.copy.wait)
        self.landed = True

    def close(self):
        self.wait()
        if self.remote and not self.left:
            when(self.out_if, self.copy.wait_send)
        self.left = True


class Transfers:
    def __init__(self, local, out, into):
        self.local, self.out, self.into = local, out, into
        self.all, self.locals, self.remotes = [], 0, 0

    def load(self, src, dst):
        copy = pltpu.make_async_copy(src, dst, self.local.at[self.locals])
        self.locals += 1
        self.all.append(Transfer(copy, False))
        return self.all[-1]

    def send(self, src, dst, peer, out_if=None, in_if=None):
        copy = pltpu.make_async_remote_copy(
            src_ref=src,
            dst_ref=dst,
            send_sem=self.out.at[self.remotes],
            recv_sem=self.into.at[self.remotes],
            device_id=peer,
            device_id_type=MESH,
        )
        self.remotes += 1
        self.all.append(Transfer(copy, True, out_if, in_if))
        return self.all[-1]

    def close(self):
        for transfer in self.all:
            transfer.close()


def rows_of(count, work, block=640):
    if count <= block or count % block:
        work(0, count)
        return

    def step(index, carry):
        work(pl.multiple_of(index * block, block), block)
        return carry

    lax.fori_loop(0, count // block, step, 0)


class Job:
    def __init__(self, plan, place, number, transfers, bufs, update):
        self.plan, self.place, self.number, self.transfers = plan, place, number, transfers
        self.own, self.send0, self.recv0, self.send, self.recv, self.full = bufs
        self.first, self.length = plan.start[number], plan.length[number]
        taps, self.order = plan.jobs[number]
        self.missing = set(taps)
        self.base, self.size = 0, self.length
        self.regions = []
        self.spare = 0
        self.waiting = []
        self.todo = [self.core] + [functools.partial(self.scatter, group) for group in self.order]
        self.todo += [self.settle]
        self.todo += [functools.partial(self.gather, group) for group in self.order[::-1]]
        self.todo += [self.gather_core, self.arrived]
        self.todo += [functools.partial(update, taps)]

    @property
    def ready(self):
        return not self.missing and bool(self.todo)

    def step(self, steps=1):
        for _ in range(steps):
            if self.ready:
                self.todo.pop(0)()

    def stored(self, tap):
        self.missing.remove(tap)
        if not self.missing:
            self.step()

    def core(self):
        rows = pl.ds(self.first, self.length)
        copy = self.transfers.send(
            self.send0.at[rows], self.recv0.at[rows], self.place.peer("c", 1)
        )
        self.waiting = [(copy, self.recv0, self.first)]

    def arrived(self):
        for copy, _, _ in self.waiting:
            copy.wait()

    def total(self, row, count):
        at = pl.multiple_of(self.first + self.base + row, 16)
        value = self.own[pl.ds(at, count)]
        for _, ref, start in self.waiting:
            value = value + ref[pl.ds(pl.multiple_of(start + row, 16), count)].astype(F32)
        return value

    def scatter(self, group):
        self.arrived()
        size = self.plan.count(group)
        part = self.size // size
        sends = []
        for distance in range(1, size):
            begin = pl.multiple_of(self.place.coord(group, distance) * part, 16)
            spot = self.first + self.spare

            def work(row, count, begin=begin, spot=spot):
                self.send[pl.ds(pl.multiple_of(spot + row, 16), count)] = self.total(
                    pl.multiple_of(begin + row, 16), count
                ).astype(BF)

            rows_of(part, work)
            rows = pl.ds(spot, part)
            copy = self.transfers.send(
                self.send.at[rows], self.recv.at[rows], self.place.peer(group, distance)
            )
            sends.append((copy, self.recv, spot))
            self.spare += part
        begin = pl.multiple_of(self.place.coord(group) * part, 16)

        def keep(row, count):
            here = pl.multiple_of(begin + row, 16)
            value = self.total(here, count)
            self.own[pl.ds(pl.multiple_of(self.first + self.base + here, 16), count)] = value

        rows_of(part, keep)
        self.base = pl.multiple_of(self.base + begin, 16)
        self.size = part
        self.regions.append((self.base, part))
        self.waiting = sends

    def settle(self):
        self.arrived()
        core = self.place.at["c"]

        def work(row, count):
            here = pl.multiple_of(self.first + self.base + row, 16)
            value = self.total(row, count)
            self.full[core, pl.ds(here, count)] = (value * jnp.abs(value)).astype(BF)

        rows_of(self.size, work)
        self.waiting = []
        self.step()

    def gather(self, group):
        self.arrived()
        core = self.place.at["c"]
        base, size = self.regions.pop()
        ref = self.full.at[core, pl.ds(pl.multiple_of(self.first + base, 16), size)]
        self.waiting = [
            (self.transfers.send(ref, ref, self.place.peer(group, distance)), None, None)
            for distance in range(1, self.plan.count(group))
        ]

    def gather_core(self):
        self.arrived()
        core = self.place.at["c"]
        ref = self.full.at[core, pl.ds(self.first, self.length)]
        self.waiting = [(self.transfers.send(ref, ref, self.place.peer("c", 1)), None, None)]


class Tiny:
    def __init__(self, plan, place, transfers, rows, slots, update):
        self.plan, self.place, self.transfers = plan, place, transfers
        self.rows, self.slots = rows, slots
        self.first, self.size, self.waiting = 0, 0, []
        self.todo = [functools.partial(self.share, dim) for dim in "cxba"] + [self.total, update]
        self.ready = False

    def step(self):
        if self.ready and self.todo:
            self.todo.pop(0)()

    def total(self):
        for copy in self.waiting:
            copy.wait()
        if self.waiting:
            self.rows[...] = sum(self.slots[self.first + index] for index in range(self.size))

    def share(self, dim):
        self.total()
        self.first += self.size
        self.size = self.plan.size[dim]
        slot = self.first + self.place.at[dim]
        self.slots[slot] = self.rows[...]
        ref = self.slots.at[slot]
        self.waiting = [
            self.transfers.send(ref, ref, self.place.peer(dim, distance))
            for distance in range(1, self.size)
        ]


def dot(a, b, dims=((1,), (0,))):
    return lax.dot_general(a, b, (dims, ((), ())), preferred_element_type=F32)


NT = ((1,), (1,))
TN = ((0,), (0,))


def shifted(value, period):
    place = lax.rem(lax.broadcasted_iota(jnp.int32, value.shape, 0), period)
    count = value.shape[0]
    on = jnp.where(place == 0, 0.0, pltpu.roll(value, 1, 0)).astype(BF)
    back = jnp.where(place == period - 1, 0.0, pltpu.roll(value, count - 1, 0)).astype(BF)
    return on, back


def level(feat_r, head_t, head_bias, target, weight, norm):
    pred = dot(head_t, feat_r, NT) + head_bias
    diff = pred - target
    size = jnp.abs(diff)
    loss = weight * jnp.where(size < BETA, 0.5 * diff * diff / BETA, size - 0.5 * BETA) / norm
    dpred = (weight * jnp.clip(diff / BETA, -1.0, 1.0) / norm).astype(BF)
    return loss, dpred


ARGS = (
    ("feats2", "feats3", "match2", "target2", "match3", "target3", "positives", "step_count"),
    ("lat2_w", "lat2_m", "lat2_v", "lat3_w", "lat3_m", "lat3_v", "conv_w", "conv_m", "conv_v"),
    ("head_w", "head_m", "head_v", "bias_w", "bias_m", "bias_v"),
)
RESULTS = (
    ("loss", "w2", "m2", "v2", "c2", "w3", "m3", "v3", "c3", "wc", "mc", "vc", "cc"),
    ("wh", "mh", "vh", "ch", "wb", "mb", "vb", "cb"),
)
SCRATCH = (
    ("own", "send0", "recv0", "send", "recv", "full", "tin", "slots"),
    ("f3", "top_s", "top_p", "strips", "x3", "d3", "k3", "t3", "q3", "tp3", "dtop_s"),
    ("f2", "up", "x2", "d2", "p2", "k2", "t2", "q2", "tt", "ww", "edge_o", "edge_i"),
    ("tl", "wl", "dpl", "lossl", "ps", "dup_f", "dup_s", "dup_r", "dm"),
    ("hp", "ht", "w2b", "local_sem", "out_sem", "in_sem"),
)


class Refs:
    def __init__(self, groups, refs):
        names = [name for group in groups for name in group]
        self.__dict__.update(zip(names, refs, strict=True))


def adamw(weight, first, second, grad, square, scale1, scale2):
    first_new = 0.9 * first + 0.1 * grad
    second_new = 0.95 * second + 0.05 * square
    weight_new = weight - 0.02 * (
        first_new * scale1 / (jnp.sqrt(second_new * scale2) + 1e-08) + 0.1 * weight
    )
    return weight_new, first_new, second_new


def main_kernel(plan, *refs):
    g = Refs(ARGS + RESULTS + SCRATCH, refs)
    place = Place(plan)
    me = place.row
    C, L = plan.width, plan.lanes
    images, rows, cols = plan.images, plan.rows, plan.cols
    H3, W3, strip = plan.high3, plan.cols3, plan.strip
    nrow = plan.nrow

    barrier = pltpu.get_barrier_semaphore()
    greeted = 0
    for distance in range(1, nrow):
        pl.semaphore_signal(
            barrier, inc=1, device_id=(place.img, place.in_row(distance)), device_id_type=MESH
        )
        greeted += 1
    for dim in "cx":
        for distance in range(1, plan.size[dim]):
            pl.semaphore_signal(
                barrier, inc=1, device_id=place.peer(dim, distance), device_id_type=MESH
            )
            greeted += 1

    transfers = Transfers(g.local_sem, g.out_sem, g.in_sem)
    load = transfers.load
    load_f3 = load(g.feats3, g.f3)
    load_w3 = load(g.lat3_w, g.w3)
    load_bias = load(g.bias_w, g.wb)
    load_head = load(g.head_w, g.wh)
    load_t3 = [load(g.target3.at[0], g.t3), load(g.match3.at[0], g.q3)]

    norm = g.positives[0].astype(F32)
    count = jnp.full((1, LANES), g.step_count[0].astype(F32))
    scale1 = (1.0 / (1.0 - jnp.exp(count * jnp.log(jnp.float32(0.9)))))[:, 0:1]
    scale2 = (1.0 / (1.0 - jnp.exp(count * jnp.log(jnp.float32(0.95)))))[:, 0:1]

    g.top_s[:, 0:8] = jnp.zeros((2, 8, LANES), F32)
    g.top_s[:, 8 + plan.cells3 : 16 + plan.cells3] = jnp.zeros((2, 8, LANES), F32)
    for ref in (g.x3, g.d3):
        ref[0] = jnp.zeros((H3, 3 * C), BF)
        ref[W3 + 1] = jnp.zeros((H3, 3 * C), BF)
    g.hp[...] = jnp.zeros(g.hp.shape, F32)
    for job, (taps, _) in enumerate(plan.jobs):
        used = len(taps) * TAP
        spare = plan.length[job] - used
        if spare:
            at = pl.ds(plan.start[job] + used, spare)
            g.own[at] = jnp.zeros((spare, LANES), F32)
            g.send0[at] = jnp.zeros((spare, LANES), BF)

    load_f3.wait()
    load_w3.wait()
    load_bias.wait()
    load_c3 = load(g.conv_w.at[1], g.wc.at[1])
    load_f2 = [load(g.feats2.at[:, f], g.f2.at[2 + f]) for f in range(rows)]
    load_w2 = load(g.lat2_w, g.w2)
    load_t2 = [load(g.target2, g.t2), load(g.match2, g.q2)]
    load_c2 = load(g.conv_w.at[0], g.wc.at[0])
    top = dot(g.f3[...], g.w3[...].astype(BF)) + g.wb[1:2]
    top = top.astype(BF).astype(F32)
    for half in range(2):
        g.top_s[half, 8 : 8 + plan.cells3] = top[:, half * LANES : (half + 1) * LANES]
    for half in range(2):
        g.top_p[:, half * LANES : (half + 1) * LANES] = g.top_s[half].astype(BF)
    pl.semaphore_wait(barrier, greeted)
    span = (strip + 2) * W3
    strip_sends = []
    for distance in range(1, nrow):
        other = place.in_row(distance)
        src = g.top_p.at[pl.ds(pl.multiple_of(other * strip * W3, 16), span)]
        strip_sends.append(transfers.send(src, g.strips.at[me], (place.img, other)))
    g.strips[me] = g.top_p[pl.ds(pl.multiple_of(me * strip * W3, 16), span)]

    has_up, has_down = me > 0, me < nrow - 1
    up_dev, down_dev = (place.img, me - 1), (place.img, me + 1)
    edge_f2 = []
    for f in range(2):
        edge_f2.append(
            transfers.send(g.feats2.at[:, f], g.f2.at[rows + 2 + f], up_dev, has_up, has_down)
        )
    for f in range(2):
        edge_f2.append(
            transfers.send(g.feats2.at[:, rows - 2 + f], g.f2.at[f], down_dev, has_down, has_up)
        )


    value = jnp.concatenate(
        [
            jnp.concatenate(
                [g.top_s[half, pl.ds(8 + col, H3, stride=W3), :] for half in range(2)], axis=1
            )
            for col in range(W3)
        ],
        axis=0,
    )

    def three(ref, low, middle, high):
        for at, value in enumerate((low, middle, high)):
            ref[1 : W3 + 1, :, at * C : (at + 1) * C] = value.reshape(W3, H3, C)

    on, back = shifted(value, H3)
    three(g.x3, on, value.astype(BF), back)
    load_c3.wait()
    for dx in range(3):
        for dy in range(3):
            tap = dy * 3 + dx
            g.k3[dx, dy * C : (dy + 1) * C] = g.wc[1, tap * C : (tap + 1) * C].astype(BF)
    load_head.wait()
    g.hp[0:12, 0 : C + 1] = g.wh[...]
    g.ht[...] = g.hp[:, 0:C].astype(BF)
    head_bias = g.hp[:, C : C + 1]
    head_t = g.ht[...]

    for copy in load_t3:
        copy.wait()
    g.tp3[...] = jnp.zeros(g.tp3.shape, F32)
    for k in range(12):
        g.tp3[0, k * W3 : (k + 1) * W3, 0:H3] = g.t3[k]
        g.tp3[1, k * W3 : (k + 1) * W3, 0:H3] = g.q3[k // 4].astype(F32)

    def coarse_rows(which):
        return jnp.concatenate(
            [g.tp3[which, pl.ds(col, 16, stride=W3), :][:, 0:H3] for col in range(W3)], axis=1
        )

    target3, weight3 = coarse_rows(0), coarse_rows(1)

    def window3(ref, dx):
        return ref[dx : dx + W3].reshape(plan.cells3, 3 * C)

    coarse = g.wb[3:4] + dot(
        jnp.concatenate([window3(g.x3, dx) for dx in range(3)], axis=1),
        g.k3[...].reshape(9 * C, C),
    )
    coarse_r = coarse.astype(BF)
    loss3, dpred3 = level(coarse_r, head_t, head_bias, target3, weight3, norm)
    head_g = dot(dpred3, coarse_r)
    hbias_g = jnp.sum(dpred3.astype(F32), axis=1, keepdims=True)
    loss = jnp.sum(loss3, axis=1, keepdims=True)
    dcoarse_r = dot(dpred3, head_t, TN).astype(BF)
    out_g3 = jnp.sum(dcoarse_r.astype(F32), axis=0, keepdims=True)
    g.tin[0:16] = head_g
    g.tin[19:20] = out_g3
    on, back = shifted(dcoarse_r.astype(F32), H3)
    three(g.d3, back, dcoarse_r, on)
    core = place.at["c"]

    arrays = {0: (g.wc, g.mc, g.vc, g.cc, 1), 9: (g.wc, g.mc, g.vc, g.cc, 0)}
    arrays |= {18: (g.w2, g.m2, g.v2, g.c2, None), 19: (g.w3, g.m3, g.v3, g.c3, None)}

    def update(taps):
        runs = []
        for tap in taps:
            first = max(start for start in arrays if start <= tap)
            if runs and runs[-1][0] == first:
                runs[-1][2] += TAP
            else:
                runs.append([first, tap, TAP])
        for first, tap, length in runs:
            *held, lead = arrays[first]

            def block(index, carry, first=first, tap=tap, held=held, lead=lead):
                row = pl.multiple_of(plan.tap_row[tap] + index * BLOCK, BLOCK)
                at = pl.ds(pl.multiple_of((tap - first) * TAP + index * BLOCK, BLOCK), BLOCK)
                for half in range(2):
                    lanes = slice(half * LANES, (half + 1) * LANES)
                    where = (at, lanes) if lead is None else (lead, at, lanes)
                    signed = g.full[half, pl.ds(row, BLOCK)].astype(F32)
                    square = jnp.abs(signed)
                    grad = jnp.sqrt(square)
                    grad = jnp.where(signed < 0.0, -grad, grad)
                    old = [ref[where] for ref in held[:3]]
                    new = adamw(*old, grad, square, scale1, scale2)
                    for ref, value in zip(held, new):
                        ref[where] = value
                    held[3][where] = new[0].astype(BF)
                return carry

            lax.fori_loop(0, length // BLOCK, block, 0)

    bufs = (g.own, g.send0, g.recv0, g.send, g.recv, g.full)
    jobs = [
        Job(plan, place, number, transfers, bufs, update) for number in range(len(plan.jobs))
    ]

    def progress(point):
        for number in SCHEDULE[point]:
            if number < len(jobs):
                jobs[number].step()

    def store_tap(tap, value):
        at = pl.ds(plan.tap_row[tap], TAP)
        left, right = value[:, 0:LANES], value[:, LANES:]
        mine = core == 0
        g.own[at] = jnp.where(mine, left, right)
        g.send0[at] = jnp.where(mine, right, left).astype(BF)
        jobs[plan.tap_job[tap]].stored(tap)

    for dx in range(3):
        grad = dot(window3(g.x3, dx), dcoarse_r, TN)
        for dy in range(3):
            store_tap(dy * 3 + dx, grad[dy * C : (dy + 1) * C])

    dtop = sum(
        dot(window3(g.d3, 2 - dx)[:, dy * C : (dy + 1) * C], g.k3[dx, dy * C : (dy + 1) * C], NT)
        for dx in range(3)
        for dy in range(3)
    )
    for col in range(W3):
        for half in range(2):
            g.dtop_s[half, pl.ds(col, H3, stride=W3), :] = dtop[
                col * H3 : (col + 1) * H3, half * LANES : (half + 1) * LANES
            ]

    late = [
        load(src, dst)
        for src, dst in (
            (g.lat2_m, g.m2),
            (g.lat2_v, g.v2),
            (g.lat3_m, g.m3),
            (g.lat3_v, g.v3),
            (g.conv_m, g.mc),
            (g.conv_v, g.vc),
            (g.head_m, g.mh),
            (g.head_v, g.vh),
            (g.bias_m, g.mb),
            (g.bias_v, g.vb),
        )
    ]

    progress("dtop3")

    for copy in load_t2:
        copy.wait()
    per = LANES // cols
    for part in range(L // LANES):
        g.tt[part] = jnp.zeros(g.tt.shape[1:], F32)
        g.ww[part] = jnp.zeros(g.ww.shape[1:], F32)
        for k in range(12):
            g.tt[part, k * rows : (k + 1) * rows] = jnp.concatenate(
                [g.t2[part * per + n, k] for n in range(per)], axis=1
            )
        for anchor in range(3):
            value = jnp.concatenate(
                [g.q2[part * per + n, anchor] for n in range(per)], axis=1
            ).astype(F32)
            for k in range(anchor * 4, anchor * 4 + 4):
                g.ww[part, k * rows : (k + 1) * rows] = value
        lanes = slice(part * LANES, (part + 1) * LANES)
        for f in range(rows):
            at = pl.ds(f, 16, stride=rows)
            g.tl[1 + f, :, lanes] = g.tt[part, at, :]
            g.wl[1 + f, :, lanes] = g.ww[part, at, :]
    g.edge_o[0, 0:16] = g.tl[1]
    g.edge_o[0, 16:32] = g.wl[1]
    g.edge_o[1, 0:16] = g.tl[rows]
    g.edge_o[1, 16:32] = g.wl[rows]

    edge_up = transfers.send(g.edge_o.at[0], g.edge_i.at[0], up_dev, has_up, has_down)
    edge_down = transfers.send(g.edge_o.at[1], g.edge_i.at[1], down_dev, has_down, has_up)
    progress("target")

    load_w2.wait()
    g.w2b[...] = g.w2[...].astype(BF)
    load_c2.wait()

    g.k2[...] = g.wc[0].astype(BF)

    for copy in load_f2:
        copy.wait()
    for copy in strip_sends:
        copy.wait()
    progress("strips")
    place_i = lax.broadcasted_iota(jnp.int32, ((strip + 2) * cols, span), 0)
    place_j = lax.broadcasted_iota(jnp.int32, ((strip + 2) * cols, span), 1)
    double = jnp.where(place_i // (cols // W3) == place_j, 1.0, 0.0).astype(BF)

    for n in range(images):
        value = dot(double, g.strips[n])
        for cr in range(strip + 2):
            g.up[cr, n] = value[cr * cols : (cr + 1) * cols]
    progress("enlarged")

    def merge(first, count, outside):
        lateral = dot(g.f2[first : first + count].reshape(count * L, C), g.w2b[...]) + g.wb[0:1]
        value = lateral + jnp.concatenate(
            [g.up[j // 2].reshape(L, C) for j in range(first, first + count)], axis=0
        )
        if outside is not None:
            value = jnp.where(outside, 0.0, value)
        value = value.astype(BF)
        on, back = shifted(value.astype(F32), cols)
        for at, part in enumerate((on, value, back)):
            g.x2[first : first + count, :, at * C : (at + 1) * C] = part.reshape(count, L, C)

    def forward(spans):
        lines = [j for first, count in spans for j in range(first, first + count)]
        cells = len(lines) * L
        fine = g.wb[2:3] + dot(
            jnp.concatenate(
                [
                    jnp.concatenate(
                        [g.x2[first + dy : first + dy + count] for first, count in spans], axis=0
                    ).reshape(cells, 3 * C)
                    for dy in range(3)
                ],
                axis=1,
            ),
            g.k2[...],
        )
        fine_r = fine.astype(BF)
        target = jnp.concatenate([g.tl[j] for j in lines], axis=1)
        weight = jnp.concatenate([g.wl[j] for j in lines], axis=1)
        loss2, dpred = level(fine_r, head_t, head_bias, target, weight, norm)
        value = dot(dpred, head_t, TN).astype(BF)
        on, back = shifted(value.astype(F32), cols)
        for at, j in enumerate(lines):
            here = slice(at * L, (at + 1) * L)
            g.p2[j] = fine_r[here]
            g.lossl[j] = loss2[:, here]
            g.dpl[j] = dpred[:, here]
            for side, part in enumerate((back, value, on)):
                g.d2[j, :, side * C : (side + 1) * C] = part[here]

    merge(2, rows, None)
    progress("merged")
    forward([(2, rows - 2)])
    progress("inner")
    for copy in edge_f2 + [edge_up, edge_down]:
        copy.wait()

    @pl.when(has_up)
    def _():
        g.tl[0] = g.edge_i[1, 0:16]
        g.wl[0] = g.edge_i[1, 16:32]

    @pl.when(me == 0)
    def _():
        g.f2[0:2] = jnp.zeros((2, images, cols, C), BF)
        g.tl[0] = jnp.zeros((16, L), F32)
        g.wl[0] = jnp.zeros((16, L), F32)

    @pl.when(has_down)
    def _():
        g.tl[rows + 1] = g.edge_i[0, 0:16]
        g.wl[rows + 1] = g.edge_i[0, 16:32]

    @pl.when(me == nrow - 1)
    def _():
        g.f2[rows + 2 : rows + 4] = jnp.zeros((2, images, cols, C), BF)
        g.tl[rows + 1] = jnp.zeros((16, L), F32)
        g.wl[rows + 1] = jnp.zeros((16, L), F32)


    merge(0, 2, me == 0)
    merge(rows + 2, 2, me == nrow - 1)
    forward([(0, 2), (rows, 2)])
    progress("forward")

    total = sum(
        dot(
            g.d2[2 - dy : 2 - dy + rows].reshape(rows * L, 3 * C)[:, dx * C : (dx + 1) * C],
            g.k2[(dy * 3 + dx) * C : (dy * 3 + dx + 1) * C],
            NT,
        )
        for dy in range(3)
        for dx in range(3)
    )
    g.dm[...] = total.astype(BF).reshape(rows, L, C)
    for q in range(strip):
        pair = total[2 * q * L : (2 * q + 1) * L] + total[(2 * q + 1) * L : (2 * q + 2) * L]
        for half in range(2):
            g.ps[q, half] = pair[:, half * LANES : (half + 1) * LANES]
            value = (
                g.ps[q, half, pl.ds(0, L // 2, stride=2), :]
                + g.ps[q, half, pl.ds(1, L // 2, stride=2), :]
            )
            g.dup_f[:, q * W3 : (q + 1) * W3, half * LANES : (half + 1) * LANES] = value.reshape(
                images, W3, LANES
            )
    g.dup_s[...] = g.dup_f[...].astype(BF)
    dup_sends = []
    for distance in range(1, nrow):
        other = place.in_row(distance)
        dup_sends.append(transfers.send(g.dup_s.at[other], g.dup_r.at[me], (place.img, other)))
    g.dup_r[me] = g.dup_s[me]
    progress("backward")

    inner = g.d2[1 : rows + 1][:, :, C : 2 * C].reshape(rows * L, C)
    for dy in range(3):
        grad = dot(g.x2[dy + 1 : dy + 1 + rows].reshape(rows * L, 3 * C), inner, TN)
        for dx in range(3):
            store_tap(9 + dy * 3 + dx, grad[dx * C : (dx + 1) * C])
        progress(("conv2a", "conv2b", "conv2")[dy])

    dpred2 = jnp.concatenate([g.dpl[1 + f] for f in range(rows)], axis=1)
    g.tin[0:16] += dot(dpred2, g.p2[1 : rows + 1].reshape(rows * L, C))
    hbias_g += jnp.sum(dpred2.astype(F32), axis=1, keepdims=True)
    loss += jnp.sum(sum(g.lossl[1 + f] for f in range(rows)), axis=1, keepdims=True)
    lane = lax.broadcasted_iota(jnp.int32, (16, LANES), 1)
    diagonal = lane == lax.broadcasted_iota(jnp.int32, (16, LANES), 0)
    g.tin[20:21, 0:LANES] = jnp.sum(jnp.where(diagonal, hbias_g, 0.0), axis=0, keepdims=True)
    g.tin[20:21, LANES:] = jnp.sum(
        jnp.broadcast_to(loss, (16, LANES)), axis=0, keepdims=True
    )
    g.tin[18:19] = jnp.sum(inner.astype(F32), axis=0, keepdims=True)
    g.tin[21:24] = jnp.zeros((3, C), F32)
    dm = g.dm[...].reshape(rows * L, C)
    store_tap(18, dot(g.f2[2 : rows + 2].reshape(rows * L, C), dm, TN))
    g.tin[16:17] = jnp.sum(dm.astype(F32), axis=0, keepdims=True)
    progress("lat2")

    for copy in dup_sends:
        copy.wait()
    dup = g.dup_r[...].reshape(plan.cells3, C).astype(F32)
    dtop = jnp.concatenate([g.dtop_s[0], g.dtop_s[1]], axis=1) + dup
    dtop_r = dtop.astype(BF)
    lat3_g = dot(g.f3[...], dtop_r, TN)
    store_tap(19, lat3_g[0:TAP])
    store_tap(20, lat3_g[TAP:])
    g.tin[17:18] = jnp.sum(dtop_r.astype(F32), axis=0, keepdims=True)
    progress("lat3")

    for copy in late:
        copy.wait()

    def update_tiny():
        hbias = jnp.sum(
            jnp.where(diagonal, jnp.broadcast_to(g.tin[20:21, 0:LANES], (16, LANES)), 0.0),
            axis=1,
            keepdims=True,
        )
        grad = jnp.concatenate([g.tin[0:12], hbias[0:12]], axis=1)
        new = adamw(g.wh[...], g.mh[...], g.vh[...], grad, grad * grad, scale1, scale2)
        for ref, value in zip((g.wh, g.mh, g.vh), new):
            ref[...] = value
        g.ch[...] = new[0].astype(BF)
        grad = g.tin[16:20]
        new = adamw(g.wb[...], g.mb[...], g.vb[...], grad, grad * grad, scale1, scale2)
        for ref, value in zip((g.wb, g.mb, g.vb), new):
            ref[...] = value
        g.cb[...] = new[0].astype(BF)
        g.loss[...] = g.tin[16:24, LANES:]

    small = Tiny(plan, place, transfers, g.tin, g.slots, update_tiny)
    small.ready = True
    while any(job.todo for job in jobs + [small]):
        small.step()
        for job in jobs:
            job.step()
    transfers.close()


def write_kernel(*refs):
    ins, outs, sem = refs[:21], refs[21:42], refs[42]
    copies = []
    for index in range(1, 21):
        src, dst = ins[index], outs[index]
        pairs = [(src, dst)]
        if len(src.shape) == 3:
            pairs = [(src.at[level], dst.at[level]) for level in range(src.shape[0])]
        for pair in pairs:
            copies.append(pltpu.make_async_copy(*pair, sem.at[len(copies)]))
            copies[-1].start()
    outs[0][0] = jnp.max(ins[0][4:5])
    for copy in copies:
        copy.wait()


def body(
    mesh_shape,
    feats2,
    feats3,
    match2,
    target2,
    match3,
    target3,
    positives,
    step_count,
    lat2_w,
    lat2_m,
    lat2_v,
    lat3_w,
    lat3_m,
    lat3_v,
    conv_w,
    conv_m,
    conv_v,
    head_w,
    head_m,
    head_v,
    bias_w,
    bias_m,
    bias_v,
):
    plan = Plan(mesh_shape, feats2.shape, feats3.shape)
    C, L, H3, W3 = plan.width, plan.lanes, plan.high3, plan.cols3
    images, rows, cols, strip, nrow = plan.images, plan.rows, plan.cols, plan.strip, plan.nrow
    head = [x.T for x in (head_w, head_m, head_v)]
    weights = [lat2_w, lat2_m, lat2_v, lat3_w, lat3_m, lat3_v, conv_w, conv_m, conv_v]
    weights += head + [bias_w, bias_m, bias_v]
    args = [
        feats2,
        feats3.reshape(plan.cells3, plan.width3),
        match2,
        target2,
        match3.transpose(0, 1, 3, 2),
        target3.transpose(0, 1, 3, 2),
    ]
    args = [pltpu.with_memory_space_constraint(x, HBM) for x in args]
    held = [pltpu.with_memory_space_constraint(x, HBM) for x in weights]
    hbm, vmem, smem = (pl.BlockSpec(memory_space=space) for space in (HBM, VMEM, SMEM))
    outs = [VMEM((8, LANES), F32)]
    for x in (lat2_w, lat3_w, conv_w, head[0], bias_w):
        outs += [VMEM(x.shape, F32)] * 3 + [VMEM(x.shape, BF)]
    span = (strip + 2) * W3
    dma = pltpu.SemaphoreType.DMA
    remotes = 2 * (nrow - 1) + 6 + plan.tiny_links + len(plan.jobs) * 2 * plan.links
    scratch = [
        VMEM((plan.total, LANES), F32),
        VMEM((plan.total, LANES), BF),
        VMEM((plan.total, LANES), BF),
        VMEM((plan.total, LANES), BF),
        VMEM((plan.total, LANES), BF),
        VMEM((2, plan.total, LANES), BF),
        VMEM((TINY, C), F32),
        VMEM((sum(plan.size.values()), TINY, C), F32),
        VMEM((plan.cells3, plan.width3), BF),
        VMEM((2, plan.cells3 + 16, LANES), F32),
        VMEM((plan.cells3 + 16, C), BF),
        VMEM((nrow, span, C), BF),
        VMEM((W3 + 2, H3, 3 * C), BF),
        VMEM((W3 + 2, H3, 3 * C), BF),
        VMEM((3, 3 * C, C), BF),
        VMEM((12, W3, H3), F32),
        VMEM((3, W3, H3), jnp.int32),
        VMEM((2, 16 * W3, LANES), F32),
        VMEM((2, plan.cells3, LANES), F32),
        VMEM((rows + 4, images, cols, C), BF),
        VMEM((strip + 2, images, cols, C), F32),
        VMEM((rows + 4, L, 3 * C), BF),
        VMEM((rows + 2, L, 3 * C), BF),
        VMEM((rows + 2, L, C), BF),
        VMEM((9 * C, C), BF),
        VMEM(target2.shape, F32),
        VMEM(match2.shape, jnp.int32),
        VMEM((L // LANES, 16 * rows, LANES), F32),
        VMEM((L // LANES, 16 * rows, LANES), F32),
        VMEM((2, 32, L), F32),
        VMEM((2, 32, L), F32),
        VMEM((rows + 2, 16, L), F32),
        VMEM((rows + 2, 16, L), F32),
        VMEM((rows + 2, 16, L), BF),
        VMEM((rows + 2, 16, L), F32),
        VMEM((strip, 2, L, LANES), F32),
        VMEM((images, strip * W3, C), F32),
        VMEM((images, strip * W3, C), BF),
        VMEM((nrow, strip * W3, C), BF),
        VMEM((rows, L, C), BF),
        VMEM((16, 3 * LANES), F32),
        VMEM((16, C), BF),
        VMEM((C, C), BF),
        dma((48,)),
        dma((remotes,)),
        dma((remotes,)),
    ]
    results = pl.pallas_call(
        functools.partial(main_kernel, plan),
        out_shape=outs,
        in_specs=[hbm] * 6 + [smem] * 2 + [hbm] * len(held),
        out_specs=[vmem] * len(outs),
        scratch_shapes=scratch,
        compiler_params=pltpu.CompilerParams(
            collective_id=0, has_side_effects=True, vmem_limit_bytes=40 << 20
        ),
        name="gradients",
    )(*args, positives.reshape(1), step_count.reshape(1), *held)
    kept = [pltpu.with_memory_space_constraint(x, VMEM) for x in results]

    shapes = [jax.ShapeDtypeStruct((1,), F32)]
    shapes += [jax.ShapeDtypeStruct(x.shape, x.dtype) for x in kept[1:]]
    new = pl.pallas_call(
        write_kernel,
        out_shape=shapes,
        in_specs=[vmem] * len(kept),
        out_specs=[smem] + [hbm] * 20,
        scratch_shapes=[dma((24,))],
        compiler_params=pltpu.CompilerParams(vmem_limit_bytes=1 << 20),
        name="results",
    )(*kept)
    outs = [new[0].reshape(())] + list(new[1:])
    for index in range(13, 17):
        outs[index] = outs[index].T
    return tuple(outs)


def solution(mesh):
    split = (
        P("img", "row", None, None),
        P(("img", "row"), None, None, None),
        P("img", None, "row", None),
        P("img", None, "row", None),
        P(("img", "row"), None, None, None),
        P(("img", "row"), None, None, None),
    )
    return jax.shard_map(
        functools.partial(body, dict(mesh.shape)),
        mesh=mesh,
        in_specs=split + (P(),) * 17,
        out_specs=(P(),) * 21,
        check_vma=False,
    )
```

time: 276 us -> 80.9 us (0.29)
  waiting for transfers between devices: 101 us -> 0 us
  Pallas kernels: 0 us -> 78.6 us
  blocking collectives: 40.2 us -> 0 us
  matrix products: 38.9 us -> 0 us
  local copies, waits for them, and re-layouts: 31.8 us -> 0 us
  starting transfers between devices: 26.1 us -> 0 us
  other arithmetic: 18.8 us -> 0 us
  between operations: 17.3 us -> 2.13 us
    psum x1 -> x0, waiting for transfers between devices: 95.3 us -> none  [body(): lax.psum((lat2_g, lat3_g, conv_g2, conv_g3, head_g, lat2_bias_g, lat3_bia...]
    pallas_call x0 -> x2, Pallas kernels: none -> 78.6 us  [the longest x1 71.2 us: body(): pl.pallas_call(functools.partial(main_kernel, plan), out_shape=outs, in_s...]
    psum x1 -> x0, blocking collectives: 40.2 us -> none  [body(): lax.psum((lat2_g, lat3_g, conv_g2, conv_g3, head_g, lat2_bias_g, lat3_bia...]
    dot_general x28 -> x0, matrix products: 30.4 us -> none  [the longest x18 19.7 us: conv_weight_grad(): jnp.einsum('nhwc,nhwo->co', window, grad_r, preferred_element_type=jnp.fl...]
    unnamed x79 -> x0, local copies, waits for them, and re-layouts: 22.6 us -> none
    convert_element_type x8 -> x0, other arithmetic: 17.8 us -> none  [the longest x5 15.3 us: adamw(): return (weight_new, first_new, second_new, weight_new.astype(jnp.bfloat16))]
    all_to_all x2 -> x0, starting transfers between devices: 13.3 us -> none  [the longest x1 7.29 us: body(): lax.all_to_all(top_r, 'row', split_axis=1, concat_axis=0, tiled=True)]
    ppermute x4 -> x0, starting transfers between devices: 12.7 us -> none  [the longest x2 6.91 us: from_behind(): return lax.ppermute(block, axis, route)]
  transfers between devices with their start and end apart: 7 -> 0, of which waited for: 2 -> 0; matrix products, arithmetic and copies ran while one was open for 16% -> 0% of each run, Pallas kernels for 0% -> 0%
where the time goes in v1:
time: 80.9 us; the launch traced here: 80.7 us
  Pallas kernels  78.6 us (97%)
  between operations  2.13 us (3%)
    pallas_call x1, Pallas kernels, body(): pl.pallas_call(functools.partial(main_kernel, plan), out_shape=outs, in_s...  71.2 us
    pallas_call x1, Pallas kernels, body(): pl.pallas_call(write_kernel, out_shape=shapes, in_specs=[vmem] * len(kept...  7.4 us

profile of v1, /device:TPU:0, one launch (start us, length us, event | category | flops | bytes accessed | tf_op | source)
XLA Modules:
  0.0 80.7 jit_solution(17453587147989481116)
XLA Ops:
  2.0 71.2 %gradients.1 = (f32[8,128]{1,0:T(8,128)S(1)}, f32[256,256]{1,0:T(8,128)S(1)}, f32[256,256]{1,0:T(8,128)S(1)}, f32[256,256]{1,0:T(8,128)S(1)}, bf16[256,256]{1,0:...) custom-call(bf16[8,8,16,256]{3,2,1,0:T(8,128)(2,1)} %refs_0_.1, ...), custom_call_target="tpu_custom_call" | custom-call | tf_op jit(solution)/shard_map/gradients/pallas_call | solution.py:958
  73.1 7.4 %results.1 = (f32[1]{0:T(128)}, f32[256,256]{1,0:T(8,128)}, f32[256,256]{1,0:T(8,128)}, f32[256,256]{1,0:T(8,128)}, bf16[256,256]{1,0:T(8,128)(2,1)}, /*index=5*...) custom-call(f32[8,128]{1,0:T(8,128)S(1)} %get-tuple-element.63.refs_, ...), custom_call_target="tpu_custom_call" | custom-call | tf_op jit(solution)/shard_map/results/pallas_call | solution.py:973

commit v2 on v1

--- a/solution.py
+++ b/solution.py
@@ -18,29 +18,8 @@
 TAP = 256
 BLOCK = 256
 TAPS = 21
-FINE_JOBS = (
-    (range(0, 5), ("x", "b", "a")),
-    (range(5, 9), ("b", "x", "a")),
-    (range(9, 12), ("x", "ba")),
-    (range(12, 15), ("b", "xa")),
-    (range(15, 18), ("x", "ba")),
-    (range(18, 21), ("b", "xa")),
-)
-SCHEDULE = {
-    "dtop3": (0, 1),
-    "target": (),
-    "strips": (0, 1),
-    "enlarged": (),
-    "merged": (),
-    "inner": (0, 1),
-    "forward": (0, 1),
-    "backward": (),
-    "conv2a": (),
-    "conv2b": (2,),
-    "conv2": (0, 1, 3),
-    "lat2": (4, 2),
-    "lat3": (0, 1, 3, 4, 2, 5),
-}
+FINE_JOBS = ((range(0,5),('xb', 'a')),(range(5,9),('xb', 'a')),(range(9,12),('xb', 'a')),(range(12,15),('xb', 'a')),(range(15,18),('xb', 'a')),(range(18,21),('xb', 'a')),)
+SCHEDULE = {'dtop3': '', 'target': '01', 'strips': '', 'enlarged': '', 'merged': '', 'inner': '', 'forward': '', 'backward': '', 'conv2a': '', 'conv2b': '0', 'conv2': '23', 'lat2': '14', 'lat3': 'tt5021t34t02513tt420530145212334545'}
 LARGE_JOBS = (
     (range(0, 8), ("x", "b", "a")),
     (range(8, 16), ("b", "x", "a")),
@@ -84,6 +63,14 @@
             number *= self.size[dim]
         return number
 
+    def crosses(self, group, distance):
+        moved = set()
+        for dim in group[::-1]:
+            step, distance = distance % self.size[dim], distance // self.size[dim]
+            if step:
+                moved.add(dim)
+        return "x" in moved and len(moved) > 1
+
 
 class Place:
     def __init__(self, plan):
@@ -201,8 +188,7 @@
         self.todo = [self.core] + [functools.partial(self.scatter, group) for group in self.order]
         self.todo += [self.settle]
         self.todo += [functools.partial(self.gather, group) for group in self.order[::-1]]
-        self.todo += [self.gather_core, self.arrived]
-        self.todo += [functools.partial(update, taps)]
+        self.todo += [self.gather_core, functools.partial(self.finish, update, taps)]
 
     @property
     def ready(self):
@@ -228,6 +214,10 @@
     def arrived(self):
         for copy, _, _ in self.waiting:
             copy.wait()
+
+    def finish(self, update, taps):
+        self.arrived()
+        update(taps)
 
     def total(self, row, count):
         at = pl.multiple_of(self.first + self.base + row, 16)
@@ -411,6 +401,14 @@
                 barrier, inc=1, device_id=place.peer(dim, distance), device_id_type=MESH
             )
             greeted += 1
+
+    for group in sorted({group for _, order in plan.jobs for group in order if len(group) > 1}):
+        for distance in range(1, plan.count(group)):
+            if plan.crosses(group, distance):
+                pl.semaphore_signal(
+                    barrier, inc=1, device_id=place.peer(group, distance), device_id_type=MESH
+                )
+                greeted += 1
 
     transfers = Transfers(g.local_sem, g.out_sem, g.in_sem)
     load = transfers.load
@@ -558,8 +556,7 @@
                     where = (at, lanes) if lead is None else (lead, at, lanes)
                     signed = g.full[half, pl.ds(row, BLOCK)].astype(F32)
                     square = jnp.abs(signed)
-                    grad = jnp.sqrt(square)
-                    grad = jnp.where(signed < 0.0, -grad, grad)
+                    grad = signed * lax.rsqrt(jnp.maximum(square, 1e-37))
                     old = [ref[where] for ref in held[:3]]
                     new = adamw(*old, grad, square, scale1, scale2)
                     for ref, value in zip(held, new):
@@ -574,10 +571,35 @@
         Job(plan, place, number, transfers, bufs, update) for number in range(len(plan.jobs))
     ]
 
+    lane = lax.broadcasted_iota(jnp.int32, (16, LANES), 1)
+    diagonal = lane == lax.broadcasted_iota(jnp.int32, (16, LANES), 0)
+
+    def update_tiny():
+        hbias = jnp.sum(
+            jnp.where(diagonal, jnp.broadcast_to(g.tin[20:21, 0:LANES], (16, LANES)), 0.0),
+            axis=1,
+            keepdims=True,
+        )
+        grad = jnp.concatenate([g.tin[0:12], hbias[0:12]], axis=1)
+        new = adamw(g.wh[...], g.mh[...], g.vh[...], grad, grad * grad, scale1, scale2)
+        for ref, value in zip((g.wh, g.mh, g.vh), new):
+            ref[...] = value
+        g.ch[...] = new[0].astype(BF)
+        grad = g.tin[16:20]
+        new = adamw(g.wb[...], g.mb[...], g.vb[...], grad, grad * grad, scale1, scale2)
+        for ref, value in zip((g.wb, g.mb, g.vb), new):
+            ref[...] = value
+        g.cb[...] = new[0].astype(BF)
+        g.loss[...] = g.tin[16:24, LANES:]
+
+    small = Tiny(plan, place, transfers, g.tin, g.slots, update_tiny)
+
     def progress(point):
-        for number in SCHEDULE[point]:
-            if number < len(jobs):
-                jobs[number].step()
+        for name in SCHEDULE[point]:
+            if name == "t":
+                small.step()
+            elif int(name) < len(jobs):
+                jobs[int(name)].step()
 
     def store_tap(tap, value):
         at = pl.ds(plan.tap_row[tap], TAP)
@@ -788,8 +810,6 @@
     g.tin[0:16] += dot(dpred2, g.p2[1 : rows + 1].reshape(rows * L, C))
     hbias_g += jnp.sum(dpred2.astype(F32), axis=1, keepdims=True)
     loss += jnp.sum(sum(g.lossl[1 + f] for f in range(rows)), axis=1, keepdims=True)
-    lane = lax.broadcasted_iota(jnp.int32, (16, LANES), 1)
-    diagonal = lane == lax.broadcasted_iota(jnp.int32, (16, LANES), 0)
     g.tin[20:21, 0:LANES] = jnp.sum(jnp.where(diagonal, hbias_g, 0.0), axis=0, keepdims=True)
     g.tin[20:21, LANES:] = jnp.sum(
         jnp.broadcast_to(loss, (16, LANES)), axis=0, keepdims=True
@@ -810,31 +830,11 @@
     store_tap(19, lat3_g[0:TAP])
     store_tap(20, lat3_g[TAP:])
     g.tin[17:18] = jnp.sum(dtop_r.astype(F32), axis=0, keepdims=True)
-    progress("lat3")
-
+    small.ready = True
     for copy in late:
         copy.wait()
-
-    def update_tiny():
-        hbias = jnp.sum(
-            jnp.where(diagonal, jnp.broadcast_to(g.tin[20:21, 0:LANES], (16, LANES)), 0.0),
-            axis=1,
-            keepdims=True,
-        )
-        grad = jnp.concatenate([g.tin[0:12], hbias[0:12]], axis=1)
-        new = adamw(g.wh[...], g.mh[...], g.vh[...], grad, grad * grad, scale1, scale2)
-        for ref, value in zip((g.wh, g.mh, g.vh), new):
-            ref[...] = value
-        g.ch[...] = new[0].astype(BF)
-        grad = g.tin[16:20]
-        new = adamw(g.wb[...], g.mb[...], g.vb[...], grad, grad * grad, scale1, scale2)
-        for ref, value in zip((g.wb, g.mb, g.vb), new):
-            ref[...] = value
-        g.cb[...] = new[0].astype(BF)
-        g.loss[...] = g.tin[16:24, LANES:]
-
-    small = Tiny(plan, place, transfers, g.tin, g.slots, update_tiny)
-    small.ready = True
+    progress("lat3")
+
     while any(job.todo for job in jobs + [small]):
         small.step()
         for job in jobs:

time: 80.9 us -> 69.3 us (0.86)
  Pallas kernels: 78.6 us -> 66.8 us
    pallas_call x1, Pallas kernels: 71.2 us -> 59.4 us  [body(): pl.pallas_call(functools.partial(main_kernel, plan), out_shape=outs, in_s...]
where the time goes in v2:
time: 69.3 us; the launch traced here: 69 us
  Pallas kernels  66.8 us (96%)
  between operations  2.13 us (3%)
    pallas_call x1, Pallas kernels, body(): pl.pallas_call(functools.partial(main_kernel, plan), out_shape=outs, in_s...  59.4 us
    pallas_call x1, Pallas kernels, body(): pl.pallas_call(write_kernel, out_shape=shapes, in_specs=[vmem] * len(kept...  7.4 us

profile of v2, /device:TPU:0, one launch (start us, length us, event | category | flops | bytes accessed | tf_op | source)
XLA Modules:
  0.0 69.0 jit_solution(6175701489236348397)
XLA Ops:
  2.0 59.4 %gradients.1 = (f32[8,128]{1,0:T(8,128)S(1)}, f32[256,256]{1,0:T(8,128)S(1)}, f32[256,256]{1,0:T(8,128)S(1)}, f32[256,256]{1,0:T(8,128)S(1)}, bf16[256,256]{1,0:...) custom-call(bf16[8,8,16,256]{3,2,1,0:T(8,128)(2,1)} %refs_0_.1, ...), custom_call_target="tpu_custom_call" | custom-call | tf_op jit(solution)/shard_map/gradients/pallas_call | solution.py:958
  61.4 7.4 %results.1 = (f32[1]{0:T(128)}, f32[256,256]{1,0:T(8,128)}, f32[256,256]{1,0:T(8,128)}, f32[256,256]{1,0:T(8,128)}, bf16[256,256]{1,0:T(8,128)(2,1)}, /*index=5*...) custom-call(f32[8,128]{1,0:T(8,128)S(1)} %get-tuple-element.63.refs_, ...), custom_call_target="tpu_custom_call" | custom-call | tf_op jit(solution)/shard_map/results/pallas_call | solution.py:973

commit v3 on v2

--- a/solution.py
+++ b/solution.py
@@ -18,8 +18,15 @@
 TAP = 256
 BLOCK = 256
 TAPS = 21
-FINE_JOBS = ((range(0,5),('xb', 'a')),(range(5,9),('xb', 'a')),(range(9,12),('xb', 'a')),(range(12,15),('xb', 'a')),(range(15,18),('xb', 'a')),(range(18,21),('xb', 'a')),)
-SCHEDULE = {'dtop3': '', 'target': '01', 'strips': '', 'enlarged': '', 'merged': '', 'inner': '', 'forward': '', 'backward': '', 'conv2a': '', 'conv2b': '0', 'conv2': '23', 'lat2': '14', 'lat3': 'tt5021t34t02513tt420530145212334545'}
+FINE_JOBS = (
+    (range(0, 5), ("xb", "a")),
+    (range(5, 9), ("xb", "a")),
+    (range(9, 12), ("xb", "a")),
+    (range(12, 15), ("xb", "a")),
+    (range(15, 19), ("xb", "a")),
+    (range(19, 21), ("xb", "a")),
+)
+SCHEDULE = {'dtop3': '', 'target': '01', 'strips': '', 'enlarged': '', 'merged': '', 'inner': '', 'forward': '', 'backward': '23', 'conv2a': '', 'conv2b': '', 'conv2': '0', 'lat2': '14', 'lat3': 'tt5021t34t02513tt420530145212334545'}
 LARGE_JOBS = (
     (range(0, 8), ("x", "b", "a")),
     (range(8, 16), ("b", "x", "a")),
@@ -770,6 +777,13 @@
     forward([(0, 2), (rows, 2)])
     progress("forward")
 
+    inner = g.d2[1 : rows + 1][:, :, C : 2 * C].reshape(rows * L, C)
+    for dy in range(3):
+        grad = dot(g.x2[dy + 1 : dy + 1 + rows].reshape(rows * L, 3 * C), inner, TN)
+        for dx in range(3):
+            store_tap(9 + dy * 3 + dx, grad[dx * C : (dx + 1) * C])
+        progress(("conv2a", "conv2b", "conv2")[dy])
+
     total = sum(
         dot(
             g.d2[2 - dy : 2 - dy + rows].reshape(rows * L, 3 * C)[:, dx * C : (dx + 1) * C],
@@ -798,13 +812,6 @@
         dup_sends.append(transfers.send(g.dup_s.at[other], g.dup_r.at[me], (place.img, other)))
     g.dup_r[me] = g.dup_s[me]
     progress("backward")
-
-    inner = g.d2[1 : rows + 1][:, :, C : 2 * C].reshape(rows * L, C)
-    for dy in range(3):
-        grad = dot(g.x2[dy + 1 : dy + 1 + rows].reshape(rows * L, 3 * C), inner, TN)
-        for dx in range(3):
-            store_tap(9 + dy * 3 + dx, grad[dx * C : (dx + 1) * C])
-        progress(("conv2a", "conv2b", "conv2")[dy])
 
     dpred2 = jnp.concatenate([g.dpl[1 + f] for f in range(rows)], axis=1)
     g.tin[0:16] += dot(dpred2, g.p2[1 : rows + 1].reshape(rows * L, C))

time: 69.3 us -> 69.1 us (level)
  no operation moved by 1% of the time
where the time goes in v3:
time: 69.1 us; the launch traced here: 68.9 us
  Pallas kernels  66.8 us (97%)
  between operations  2.13 us (3%)
    pallas_call x1, Pallas kernels, body(): pl.pallas_call(functools.partial(main_kernel, plan), out_shape=outs, in_s...  59.4 us
    pallas_call x1, Pallas kernels, body(): pl.pallas_call(write_kernel, out_shape=shapes, in_specs=[vmem] * len(kept...  7.4 us

profile of v3, /device:TPU:0, one launch (start us, length us, event | category | flops | bytes accessed | tf_op | source)
XLA Modules:
  0.0 68.9 jit_solution(9382651322027136556)
XLA Ops:
  2.0 59.4 %gradients.1 = (f32[8,128]{1,0:T(8,128)S(1)}, f32[256,256]{1,0:T(8,128)S(1)}, f32[256,256]{1,0:T(8,128)S(1)}, f32[256,256]{1,0:T(8,128)S(1)}, bf16[256,256]{1,0:...) custom-call(bf16[8,8,16,256]{3,2,1,0:T(8,128)(2,1)} %refs_0_.1, ...), custom_call_target="tpu_custom_call" | custom-call | tf_op jit(solution)/shard_map/gradients/pallas_call | solution.py:965
  61.4 7.4 %results.1 = (f32[1]{0:T(128)}, f32[256,256]{1,0:T(8,128)}, f32[256,256]{1,0:T(8,128)}, f32[256,256]{1,0:T(8,128)}, bf16[256,256]{1,0:T(8,128)(2,1)}, /*index=5*...) custom-call(f32[8,128]{1,0:T(8,128)S(1)} %get-tuple-element.63.refs_, ...), custom_call_target="tpu_custom_call" | custom-call | tf_op jit(solution)/shard_map/results/pallas_call | solution.py:980
